TPU v7x, 32 devices: a whole 2x2x4 slice. The times are simulated.
32 devices in a mesh: depth: 8 (over z, y), tile: 4 (over x, core).
Axes of the slice: x: 2, y: 2, z: 4, core: 2. Of those that a mesh axis runs over, the one named last changes fastest.
Arguments:
- ensemble: bfloat16 [64, 8, 64, 8192], P('tile', None, 'depth'), may hold values from -8 to 8
- active: int32 [8, 64], P('depth'), may hold values from 0 to 1, as said below
- depth_rank: int32 [8], replicated, may hold values from 0 to 7, as said below
Outputs:
- picture: float32 [4, 4, 65536], P(None, 'tile', 'depth')
Inputs may be any that keep to these rules, and one draw needn't show every extreme that they name: Every slab has exactly 32 active bricks. depth_rank[s] = s XOR k for one integer k.
All inputs are finite; a program needn't handle non-finite values.
Results may differ from a plain program's by a relative error of at most 0.0003.
Values may be sent and summed in bfloat16 or wider, within the bound.
A program may use at most 128 MiB of HBM per device.

v0:
```python
import jax
import jax.numpy as jnp
from jax import lax
from jax.sharding import PartitionSpec as P

BZ = 2


SHARPNESS = 4.0
ISOVALUE = 0.25
DENSITY = 0.35


def swapped(x, axis, apart):
    return lax.ppermute(x, axis, [(i, i ^ 1 << apart) for i in range(lax.axis_size(axis))])


def illuminate(mean_field, variance, above_prob):
    spread = jnp.sqrt(variance + 1e-06)
    depth_sum = jnp.cumsum(above_prob, axis=-2)
    transmit = jnp.exp(-DENSITY * (depth_sum - above_prob))
    weight = transmit * (1.0 - jnp.exp(-DENSITY * above_prob))
    red_sum = jnp.sum(weight * jax.nn.sigmoid(2.0 * mean_field), axis=-2)
    green_sum = jnp.sum(weight * (spread / (1.0 + spread)), axis=-2)
    blue_sum = jnp.sum(weight * above_prob, axis=-2)
    opacity = 1.0 - jnp.exp(-DENSITY * depth_sum[..., -1, :])
    return jnp.stack([red_sum, green_sum, blue_sum, opacity])


def render_members(samples):
    mean_field = jnp.mean(samples, axis=0)
    variance = jnp.mean((samples - mean_field) ** 2, axis=0)
    above_prob = jnp.mean(jax.nn.sigmoid(SHARPNESS * (samples - ISOVALUE)), axis=0)
    return illuminate(mean_field, variance, above_prob)


def body(ensemble, active, depth_rank):
    tile_count = lax.axis_size("tile")
    tile_id = lax.axis_index("tile")
    depth_count = lax.axis_size("depth")
    depth_id = lax.axis_index("depth")
    cells = ensemble.shape[3]
    brick_total = active.shape[1]
    per_tile = brick_total // tile_count
    pixels = cells // BZ
    flag_row = active[0]
    own_flags = lax.dynamic_slice_in_dim(flag_row, tile_id * per_tile, per_tile).astype(jnp.float32)
    regrouped = lax.all_to_all(
        lax.all_to_all(ensemble, "depth", split_axis=1, concat_axis=2, tiled=True),
        "tile",
        split_axis=2,
        concat_axis=0,
        tiled=True,
    )
    samples = regrouped.astype(jnp.float32).reshape(regrouped.shape[0], per_tile, BZ, pixels)
    shaded = render_members(samples) * own_flags[None, :, None]
    block_len = per_tile * pixels // depth_count
    image_rows = shaded.reshape(4, depth_count, block_len)
    own_rank = depth_rank[depth_id]
    current = image_rows
    for section in range(depth_count.bit_length() - 1):
        paired = current.reshape(4, current.shape[1] // 2, 2, block_len)
        my_bit = depth_id >> section & 1
        kept = jnp.where(my_bit == 1, paired[:, :, 1], paired[:, :, 0])
        handed = jnp.where(my_bit == 1, paired[:, :, 0], paired[:, :, 1])
        partner = swapped(handed, "depth", section)
        partner_rank = depth_rank[depth_id ^ 1 << section]
        mine_front = own_rank < partner_rank
        front_part = jnp.where(mine_front, kept, partner)
        back_part = jnp.where(mine_front, partner, kept)
        current = front_part + (1.0 - front_part[3:4]) * back_part
    return current


def solution(mesh):
    in_specs = (P("tile", None, "depth", None), P("depth", None), P())
    out_specs = P(None, "tile", "depth")
    return jax.shard_map(body, mesh=mesh, in_specs=in_specs, out_specs=out_specs, check_vma=False)
```

profile of v0, /device:TPU:6, one launch (start us, length us, event | category | flops | bytes accessed | tf_op | source)
XLA Modules:
  0.0 661.8 jit_solution(898726807793159516)
XLA Ops:
  0.0 8.5 %copy.45 = bf16[16,8,8,8192]{3,2,0,1:T(8,128)(2,1)S(1)} copy(bf16[16,8,8,8192]{3,2,1,0:T(8,128)(2,1)} %param.3) | data formatting | bytes 33554432 | tf_op args[0]
  8.5 368.4 %all_to_all.21 = bf16[16,8,8,8192]{3,2,0,1:T(8,128)(2,1)S(1)} all-to-all(bf16[16,8,8,8192]{3,2,0,1:T(8,128)(2,1)S(1)} %copy.45), channel_id=1, replica_groups=mesh['depth'=8,'tile'=4] {'depth'}, dimensions={1} | all-to-all | bytes 33554432 | tf_op jit(solution)/shard_map/all_to_all | solution.py:49
  376.9 2.2 copy.77
  379.1 25.1 %copy.47 = bf16[16,1,64,8192]{3,0,1,2:T(8,128)(2,1)} copy(bf16[16,1,64,8192]{3,2,0,1:T(8,128)(2,1)S(1)} %bitcast.87) | data formatting | bytes 33554432 | tf_op jit(solution)/shard_map/all_to_all | solution.py:49
  404.2 7.6 %all-to-all-start.1 = ((bf16[16,1,64,8192]{3,0,1,2:T(8,128)(2,1)}), bf16[16,1,64,8192]{3,0,1,2:T(8,128)(2,1)}, u32[]{:S(2)}, u32[]{:S(2)}) async-start(bf16[16,1,64,8192]{3,0,1,2:T(8,128)(2,1)} %copy.47), calls=%async_computation.1 | async-start | bytes 33554432 | tf_op jit(solution)/shard_map/all_to_all | solution.py:48
  412.5 180.8 %all-to-all-done.1 = bf16[16,1,64,8192]{3,0,1,2:T(8,128)(2,1)} async-done(((bf16[16,1,64,8192]{3,0,1,2:T(8,128)(2,1)}), bf16[16,1,64,8192]{3,0,1,2:T(8,128)(2,1)}, u32[]{:S(2)}, u32[]{:S(2)}) %all-to-all-start.1) | async-done | bytes 16777248 | tf_op jit(solution)/shard_map/all_to_all | solution.py:48
  593.3 7.0 %fusion.1 = f32[16,8192]{1,0:T(8,128)S(1)} fusion(bf16[16,1,4,16,8192]{4,0,3,2,1:T(8,128)(2,1)} %bitcast.6), kind=kLoop, calls=%fused_computation.2 | loop fusion | flops 16646144 | bytes 17301504 | tf_op jit(solution)/shard_map/reduce_sum | solution.py:31
  600.4 16.0 %fusion.9 = (f32[16,8192]{1,0:T(8,128)S(1)}, f32[16,8192]{1,0:T(8,128)S(1)}) fusion(bf16[16,1,4,16,8192]{4,0,3,2,1:T(8,128)(2,1)} %bitcast.6, f32[16,8192]{1,0:T(8,128)S(1)} %get-tuple-element.14), kind=kLoop, calls=%fused_computation.10 | loop fusion | flops 83623936 | bytes 18350080 | tf_op jit(solution)/shard_map/reduce_sum | solution.py:32
  617.6 0.4 sub.60
  618.5 2.7 reduce_window_sum.11
  621.2 1.0 fusion.16
  622.2 3.5 multiply_reduce_fusion.1
  625.7 1.1 stack.13
  626.8 1.1 stack.14
  628.3 0.5 maximum_multiply_fusion
  628.8 1.0 fusion.21
  630.2 0.6 collective-permute-start
  630.8 0.7 fusion.22
  632.8 11.2 %collective-permute-done = f32[4,4,8192]{2,1,0:T(4,128)S(1)} collective-permute-done((f32[4,4,8192]{2,1,0:T(4,128)S(1)}, f32[4,4,8192]{2,1,0:T(4,128)S(1)}, u32[]{:S(2)}, u32[]{:S(2)}) %collective-permute-start) | collective-permute-done | bytes 524320 | tf_op jit(solution)/shard_map/ppermute | solution.py:15
  644.0 0.7 broadcast_select_fusion.1
  644.7 0.7 multiply_add_fusion
  647.2 6.0 collective-permute-done.1
  655.2 5.6 collective-permute-done.2
  661.0 0.8 copy.57
  (29 shorter events, 4.4 us)
Async XLA Ops:
  404.2 7.6 %copy-start.1 = (s32[1,64]{1,0:T(1,128)S(1)}, s32[1,64]{1,0:T(1,128)}, u32[]{:S(2)}) copy-start(s32[1,64]{1,0:T(1,128)} %param.4) | copy-start | bytes 772
  404.2 189.0 %all-to-all-start.1 = ((bf16[16,1,64,8192]{3,0,1,2:T(8,128)(2,1)}), bf16[16,1,64,8192]{3,0,1,2:T(8,128)(2,1)}, u32[]{:S(2)}, u32[]{:S(2)}) async-start(bf16[16,1,64,8192]{3,0,1,2:T(8,128)(2,1)} %copy.47), calls=%async_computation.1 | async-start | bytes 33554432 | tf_op jit(solution)/shard_map/all_to_all | solution.py:48
  600.4 30.4 %copy-start = (s32[8]{0:T(128)S(1)}, s32[8]{0:T(128)}, u32[]{:S(2)}) copy-start(s32[8]{0:T(128)} %param.5) | copy-start | bytes 100
  630.2 13.8 %collective-permute-start = (f32[4,4,8192]{2,1,0:T(4,128)S(1)}, f32[4,4,8192]{2,1,0:T(4,128)S(1)}, u32[]{:S(2)}, u32[]{:S(2)}) collective-permute-start(f32[4,4,8192]{2,1,0:T(4,128)S(1)} %bitcast.91), channel_id=1, source_target_pairs={{0,4},{4,0},{8,12},{12,8},{16,20},{20,16},{24,28},{28,24},{1,5},{5... | collective-permute-start | bytes 1572872 | tf_op jit(solution)/shard_map/ppermute | solution.py:15
  645.8 7.3 %collective-permute-start.1 = (f32[4,2,8192]{2,0,1:T(4,128)S(1)}, f32[4,2,8192]{2,0,1:T(4,128)S(1)}, u32[]{:S(2)}, u32[]{:S(2)}) collective-permute-start(f32[4,2,8192]{2,0,1:T(4,128)S(1)} %select_bitcast_fusion), channel_id=1, source_target_pairs={{0,8},{4,12},{8,0},{12,4},{16,24},{20,28},{24,16},{28,20},{1,9},{5... | collective-permute-start | bytes 786440 | tf_op jit(solution)/shard_map/ppermute | solution.py:15
  653.6 7.3 %collective-permute-start.2 = (f32[4,1,8192]{2,0,1:T(4,128)S(1)}, f32[4,1,8192]{2,0,1:T(4,128)S(1)}, u32[]{:S(2)}, u32[]{:S(2)}) collective-permute-start(f32[4,1,8192]{2,0,1:T(4,128)S(1)} %select_bitcast_fusion.1), channel_id=1, source_target_pairs={{0,16},{4,20},{8,24},{12,28},{16,0},{20,4},{24,8},{28,12},{1,17},{... | collective-permute-start | bytes 393224 | tf_op jit(solution)/shard_map/ppermute | solution.py:15
where the time goes:
time: 664 us; the launch traced here: 662 us
  blocking collectives  368 us (55%)
  waiting for transfers between devices  204 us (31%)
  local copies, waits for them, and re-layouts  42.9 us (6%)
  other arithmetic  34.2 us (5%)
  starting transfers between devices  8.59 us (1%)
    all_to_all x1, blocking collectives, body(): lax.all_to_all(ensemble, 'depth', split_axis=1, concat_axis=2, tiled=True)  368 us
    all_to_all x1, waiting for transfers between devices, body(): lax.all_to_all(lax.all_to_all(ensemble, 'depth', split_axis=1, concat_axi...  181 us
    all_to_all x2, local copies, waits for them, and re-layouts, body(): lax.all_to_all(ensemble, 'depth', split_axis=1, concat_axis=2, tiled=True)  27.3 us
    ppermute x3, waiting for transfers between devices, swapped(): lax.ppermute(x, axis, [(i, i ^ 1 << apart) for i in range(lax.axis_size(a...  22.8 us
    reduce_sum x1, other arithmetic, render_members(): variance = jnp.mean((samples - mean_field) ** 2, axis=0)  16 us
  transfers between devices with their start and end apart: 4, of which 4 were waited for; matrix products, arithmetic and copies ran while one was open for 0% of the time, Pallas kernels for 0%

commit v1 on v0

v1 whole, which is shorter than its diff:
```python
import functools

import jax
import jax.numpy as jnp
from jax import lax
from jax.experimental import pallas as pl
from jax.experimental.pallas import tpu as pltpu
from jax.sharding import PartitionSpec as P

BZ = 2
CORES = 2
SHARPNESS = 4.0
ISOVALUE = 0.25
DENSITY = 0.35
FIELD_MAX = 8.0
CODE_MAX = 65535.0
MEAN_STEP = 2.0 * FIELD_MAX / CODE_MAX
ROOT_STEP = FIELD_MAX**0.5 / CODE_MAX
PROB_STEP = 1.0 / CODE_MAX
LANES = 256


def fourth_root(x):
    return jnp.sqrt(jnp.sqrt(x))


def to_code(x, step):
    return jnp.clip(x * (1.0 / step) + 0.5, 0.0, CODE_MAX).astype(jnp.int32)


def pair(low, high):
    return low | (high << 16)


def unpair(word):
    low = word & 0xFFFF
    high = lax.shift_right_logical(word, jnp.full_like(word, 16))
    return low.astype(jnp.float32), high.astype(jnp.float32)


def kernel(
    geo, ens, active, rank, out,
    held, abuf, bbuf, sibling, own, xsend, xrecv, flags, layers, rows,
    load_sem, asend_sem, arecv_sem, xsend_sem, xrecv_sem, fsend_sem, frecv_sem, osend_sem, orecv_sem, local_sem,
):
    slabs, members, bricks, pixels, depth_n, tile_n, per_tile = geo
    chips = tile_n // CORES
    width = pixels // tile_n
    lanes = min(LANES, width)
    chunks = width // lanes
    per_out = per_tile // depth_n
    d = lax.axis_index("depth")
    t = lax.axis_index("tile")
    x = t // CORES
    core = t % CORES

    def load(s):
        return pltpu.make_async_copy(ens.at[:, s], held.at[s], load_sem.at[s])

    for s in range(slabs):
        load(s).start()

    first = d * bricks
    goal_tile = first // per_tile
    goal_depth = (first % per_tile) // per_out
    my_first = t * per_tile + d * per_out
    source_depth = my_first // bricks
    same = source_depth == d
    barrier = pltpu.get_barrier_semaphore()

    def greet(depth, tile):
        pl.semaphore_signal(
            barrier, inc=1, device_id=(depth, tile), device_id_type=pl.DeviceIdType.MESH
        )

    greet(d, x * CORES + 1 - core)
    for j in range(1, chips):
        greet(d, ((x + j) % chips) * CORES + core)
    for j in range(1, depth_n):
        greet((d + j) % depth_n, t)
    goals = bricks // per_out
    for u in range(goals):
        @pl.when(jnp.logical_not(jnp.logical_and(goal_depth + u == d, goal_tile == t)))
        def _():
            greet(goal_depth + u, goal_tile)
    for u in range(tile_n):
        @pl.when(jnp.logical_not(jnp.logical_and(same, t == u)))
        def _():
            greet(source_depth, jnp.int32(u))

    def partial(s, side, store):
        def step(i, carry):
            region = i // chunks
            base = (region // BZ * CORES + side) * width + region % BZ * pixels
            column = pl.multiple_of(base + i % chunks * lanes, lanes)
            samples = [held[s, m, :, pl.ds(column, lanes)].astype(jnp.float32) for m in range(members)]
            total = samples[0]
            for v in samples[1:]:
                total = total + v
            mean = total * (1.0 / members)
            square = None
            above = None
            for v in samples:
                c = v - mean
                c = c * c
                h = jnp.tanh(v * (0.5 * SHARPNESS) - 0.5 * SHARPNESS * ISOVALUE)
                square = c if square is None else square + c
                above = h if above is None else above + h
            at = pl.ds(pl.multiple_of(i * lanes, lanes), lanes)
            store(0, at, mean)
            store(1, at, square * (1.0 / members))
            store(2, at, above * (0.5 / members) + 0.5)
            return carry

        lax.fori_loop(0, chips * BZ * chunks, step, 0)

    def store_a(s):
        def store(q, at, value):
            abuf[s, q, :, at] = value
        return store

    def store_b(q, at, value):
        bbuf[q, :, at] = value

    def to_sibling(s):
        return pltpu.make_async_remote_copy(
            src_ref=abuf.at[s], dst_ref=sibling.at[s],
            send_sem=asend_sem.at[s], recv_sem=arecv_sem.at[s],
            device_id=(d, x * CORES + 1 - core), device_id_type=pl.DeviceIdType.MESH,
        )

    def to_chip(s, j):
        return pltpu.make_async_remote_copy(
            src_ref=xsend.at[s, j - 1], dst_ref=xrecv.at[s, j - 1],
            send_sem=xsend_sem.at[s, j - 1], recv_sem=xrecv_sem.at[s, j - 1],
            device_id=(d, (x + j) % chips * CORES + core), device_id_type=pl.DeviceIdType.MESH,
        )

    def to_depth(j):
        return pltpu.make_async_remote_copy(
            src_ref=active, dst_ref=flags.at[d],
            send_sem=fsend_sem.at[j - 1], recv_sem=frecv_sem.at[j - 1],
            device_id=((d + j) % depth_n, t), device_id_type=pl.DeviceIdType.MESH,
        )

    def from_depth(j):
        return pltpu.make_async_remote_copy(
            src_ref=active, dst_ref=flags.at[(d + depth_n - j) % depth_n],
            send_sem=fsend_sem.at[j - 1], recv_sem=frecv_sem.at[j - 1],
            device_id=((d + j) % depth_n, t), device_id_type=pl.DeviceIdType.MESH,
        )

    def merged(s, at):
        ma, va, pa = (bbuf[q, :, at] for q in range(3))
        mb, vb, pb = (sibling[s, q, :, at] for q in range(3))
        gap = ma - mb
        return (ma + mb) * 0.5, (va + vb) * 0.5 + gap * gap * 0.25, (pa + pb) * 0.5

    def combine(s):
        for j in list(range(1, chips)) + [0]:
            other = (x + j) % chips

            def step(i, carry, j=j, other=other):
                at = pl.ds(pl.multiple_of(i * lanes, lanes), lanes)
                found = []
                for z in range(BZ):
                    base = (other * BZ + z) * width + i * lanes
                    found.append(merged(s, pl.ds(pl.multiple_of(base, lanes), lanes)))
                if j == 0:
                    for z in range(BZ):
                        for q in range(3):
                            own[s, z * 3 + q, :, at] = found[z][q]
                else:
                    (m0, v0, p0), (m1, v1, p1) = found
                    xsend[s, j - 1, 0, :, at] = pair(
                        to_code(m0 + FIELD_MAX, MEAN_STEP), to_code(m1 + FIELD_MAX, MEAN_STEP)
                    )
                    xsend[s, j - 1, 1, :, at] = pair(
                        to_code(fourth_root(v0), ROOT_STEP), to_code(fourth_root(v1), ROOT_STEP)
                    )
                    xsend[s, j - 1, 2, :, at] = pair(
                        to_code(fourth_root(p0), PROB_STEP), to_code(fourth_root(p1), PROB_STEP)
                    )
                return carry

            lax.fori_loop(0, chunks, step, 0)
            if j:
                to_chip(s, j).start()

    total_bricks = active.shape[1]

    def finalize(s):
        for j in range(1, chips):
            to_chip(s, j).wait_recv()
        row = flags[s]
        lane = lax.broadcasted_iota(jnp.int32, (bricks, total_bricks), 1)
        brick = lax.broadcasted_iota(jnp.int32, (bricks, total_bricks), 0)
        picked = jnp.where(lane == brick + first, row.astype(jnp.float32), 0.0)
        shown = jnp.sum(picked, axis=1, keepdims=True)

        def step(i, carry):
            at = pl.ds(pl.multiple_of(i * lanes, lanes), lanes)
            means, variances, probs = ([[own[s, z * 3 + q, :, at]] for z in range(BZ)] for q in range(3))
            for j in range(chips - 1):
                for z, code in enumerate(unpair(xrecv[s, j, 0, :, at])):
                    means[z].append(code * MEAN_STEP - FIELD_MAX)
                for z, code in enumerate(unpair(xrecv[s, j, 1, :, at])):
                    root = code * ROOT_STEP
                    variances[z].append(root * root * (root * root))
                for z, code in enumerate(unpair(xrecv[s, j, 2, :, at])):
                    root = code * PROB_STEP
                    probs[z].append(root * root * (root * root))
            mean, spread, prob = [], [], []
            for z in range(BZ):
                m = sum(means[z][1:], means[z][0]) * (1.0 / chips)
                v = sum(variances[z][1:], variances[z][0])
                for part in means[z]:
                    v = v + (part - m) * (part - m)
                mean.append(m)
                spread.append(jnp.sqrt(v * (1.0 / chips) + 1e-06))
                prob.append(sum(probs[z][1:], probs[z][0]) * (1.0 / chips))
            clear = [jnp.exp(-DENSITY * p) for p in prob]
            weight = [1.0 - clear[0], clear[0] * (1.0 - clear[1])]
            red = green = blue = 0.0
            for z in range(BZ):
                red = red + weight[z] * (0.5 + 0.5 * jnp.tanh(mean[z]))
                green = green + weight[z] * (spread[z] / (1.0 + spread[z]))
                blue = blue + weight[z] * prob[z]
            opacity = 1.0 - jnp.exp(-DENSITY * (prob[0] + prob[1]))
            for c, value in enumerate((red, green, blue, opacity)):
                layers[s, c, :, at] = value * shown
            return carry

        lax.fori_loop(0, chunks, step, 0)

    load(0).wait()
    partial(0, 1 - core, store_a(0))
    pl.semaphore_wait(
        barrier, chips + depth_n - 1 + goals + tile_n - 2 * same.astype(jnp.int32)
    )
    to_sibling(0).start()
    for j in range(1, depth_n):
        to_depth(j).start()
    mine = pltpu.make_async_copy(active, flags.at[d], local_sem.at[bricks])
    mine.start()
    mine.wait()

    def slab_step(s, carry):
        partial(s, core, store_b)

        @pl.when(s < slabs - 1)
        def _():
            load(s + 1).wait()
            partial(s + 1, 1 - core, store_a(s + 1))
            to_sibling(s + 1).start()

        to_sibling(s).wait_recv()
        combine(s)

        @pl.when(s == 0)
        def _():
            for j in range(1, depth_n):
                from_depth(j).wait_recv()

        @pl.when(s > 0)
        def _():
            finalize(s - 1)

        return carry

    lax.fori_loop(0, slabs, slab_step, 0)
    finalize(slabs - 1)

    flip = rank[0]

    def blend(i, carry):
        at = pl.ds(pl.multiple_of(i * lanes, lanes), lanes)

        def over(r, picture):
            slab = lax.bitwise_xor(r, flip)
            through = 1.0 - picture[3]
            return tuple(picture[c] + through * layers[slab, c, :, at] for c in range(4))

        picture = lax.fori_loop(0, slabs, over, tuple(jnp.zeros((bricks, lanes), jnp.float32) for _ in range(4)))
        for b in range(bricks):
            for c in range(4):
                rows[b, c : c + 1, at] = picture[c][b : b + 1, :]
        return carry

    lax.fori_loop(0, chunks, blend, 0)

    def place(tile, slot):
        return out.at[:, pl.ds(pl.multiple_of(slot * pixels + tile * width, width), width)]

    def is_self(b):
        return jnp.logical_and(goal_depth + b // per_out == d, goal_tile == t)

    def keep(b):
        return pltpu.make_async_copy(rows.at[b], place(t, b % per_out), local_sem.at[b])

    def hand(b):
        return pltpu.make_async_remote_copy(
            src_ref=rows.at[b], dst_ref=place(t, b % per_out),
            send_sem=osend_sem.at[b], recv_sem=orecv_sem.at[t, b % per_out],
            device_id=(goal_depth + b // per_out, goal_tile), device_id_type=pl.DeviceIdType.MESH,
        )

    for b in range(bricks):
        @pl.when(is_self(b))
        def _():
            keep(b).start()

        @pl.when(jnp.logical_not(is_self(b)))
        def _():
            hand(b).start()

    for b in range(bricks):
        @pl.when(is_self(b))
        def _():
            keep(b).wait()

        @pl.when(jnp.logical_not(is_self(b)))
        def _():
            hand(b).wait_send()

    for u in range(tile_n):
        @pl.when(jnp.logical_not(jnp.logical_and(same, t == u)))
        def _():
            for slot in range(per_out):
                pltpu.make_async_remote_copy(
                    src_ref=rows.at[slot], dst_ref=place(u, slot),
                    send_sem=osend_sem.at[slot], recv_sem=orecv_sem.at[u, slot],
                    device_id=(source_depth, jnp.int32(u)), device_id_type=pl.DeviceIdType.MESH,
                ).wait_recv()

    def drain(s, carry):
        to_sibling(s).wait_send()
        for j in range(1, chips):
            to_chip(s, j).wait_send()
        return carry

    lax.fori_loop(0, slabs, drain, 0)
    for j in range(1, depth_n):
        to_depth(j).wait_send()


def body(ensemble, active, depth_rank):
    tile_n = lax.axis_size("tile")
    depth_n = lax.axis_size("depth")
    members, slabs, bricks, cells = ensemble.shape
    pixels = cells // BZ
    per_tile = active.shape[1] // tile_n
    per_out = per_tile // depth_n
    chips = tile_n // CORES
    width = pixels // tile_n
    geo = (slabs, members, bricks, pixels, depth_n, tile_n, per_tile)
    f32, i32 = jnp.float32, jnp.int32
    side = chips * BZ * width
    dma = pltpu.SemaphoreType.DMA
    picture = pl.pallas_call(
        functools.partial(kernel, geo),
        out_shape=jax.ShapeDtypeStruct((4, per_out * pixels), f32),
        in_specs=[
            pl.BlockSpec(memory_space=pl.ANY),
            pl.BlockSpec(memory_space=pltpu.VMEM),
            pl.BlockSpec(memory_space=pltpu.SMEM),
        ],
        out_specs=pl.BlockSpec(memory_space=pltpu.VMEM),
        scratch_shapes=[
            pltpu.VMEM((slabs, members, bricks, cells), jnp.bfloat16),
            pltpu.VMEM((slabs, 3, bricks, side), f32),
            pltpu.VMEM((3, bricks, side), f32),
            pltpu.VMEM((slabs, 3, bricks, side), f32),
            pltpu.VMEM((slabs, 3 * BZ, bricks, width), f32),
            pltpu.VMEM((slabs, chips - 1, 3, bricks, width), i32),
            pltpu.VMEM((slabs, chips - 1, 3, bricks, width), i32),
            pltpu.VMEM((depth_n, 1, active.shape[1]), i32),
            pltpu.VMEM((slabs, 4, bricks, width), f32),
            pltpu.VMEM((bricks, 4, width), f32),
            dma((slabs,)),
            dma((slabs,)),
            dma((slabs,)),
            dma((slabs, chips - 1)),
            dma((slabs, chips - 1)),
            dma((depth_n - 1,)),
            dma((depth_n - 1,)),
            dma((bricks,)),
            dma((tile_n, per_out)),
            dma((bricks + 1,)),
        ],
        compiler_params=pltpu.CompilerParams(
            collective_id=0, has_side_effects=True, vmem_limit_bytes=56 * 1024 * 1024
        ),
    )(ensemble, active, depth_rank)
    return picture[:, None, :]


def solution(mesh):
    in_specs = (P("tile", None, "depth", None), P("depth", None), P())
    out_specs = P(None, "tile", "depth")
    return jax.shard_map(body, mesh=mesh, in_specs=in_specs, out_specs=out_specs, check_vma=False)
```

time: 664 us -> 42 us (0.06)
  blocking collectives: 368 us -> 0 us
  waiting for transfers between devices: 204 us -> 0 us
  local copies, waits for them, and re-layouts: 42.9 us -> 1.69 us
  Pallas kernels: 0 us -> 40.2 us
  other arithmetic: 34.2 us -> 0 us
  starting transfers between devices: 8.59 us -> 0 us
    all_to_all x1 -> x0, blocking collectives: 368 us -> none  [body(): lax.all_to_all(ensemble, 'depth', split_axis=1, concat_axis=2, tiled=True)]
    all_to_all x1 -> x0, waiting for transfers between devices: 181 us -> none  [body(): lax.all_to_all(lax.all_to_all(ensemble, 'depth', split_axis=1, concat_axi...]
    pallas_call x0 -> x1, Pallas kernels: none -> 40.2 us  [body(): pl.pallas_call(functools.partial(kernel, geo), out_shape=jax.ShapeDtypeSt...]
    all_to_all x2 -> x0, local copies, waits for them, and re-layouts: 27.3 us -> none  [body(): lax.all_to_all(ensemble, 'depth', split_axis=1, concat_axis=2, tiled=True)]
    reduce_sum x3 -> x0, other arithmetic: 26.5 us -> none  [the longest x1 16 us: render_members(): variance = jnp.mean((samples - mean_field) ** 2, axis=0)]
    ppermute x3 -> x0, waiting for transfers between devices: 22.8 us -> none  [swapped(): lax.ppermute(x, axis, [(i, i ^ 1 << apart) for i in range(lax.axis_size(a...]
    unnamed x7 -> x0, local copies, waits for them, and re-layouts: 8.92 us -> none
    all_to_all x1 -> x0, starting transfers between devices: 7.58 us -> none  [body(): lax.all_to_all(lax.all_to_all(ensemble, 'depth', split_axis=1, concat_axi...]
  transfers between devices with their start and end apart: 4 -> 0, of which waited for: 4 -> 0; matrix products, arithmetic and copies ran while one was open for 0% -> 0% of each run, Pallas kernels for 0% -> 0%
where the time goes in v1:
time: 42 us; the launch traced here: 41.9 us
  Pallas kernels  40.2 us (96%)
  local copies, waits for them, and re-layouts  1.69 us (4%)
    pallas_call x1, Pallas kernels, body(): pl.pallas_call(functools.partial(kernel, geo), out_shape=jax.ShapeDtypeSt...  40.2 us
    broadcast_in_dim x1, local copies, waits for them, and re-layouts, body(): return picture[:, None, :]  1.69 us

profile of v1, /device:TPU:6, one launch (start us, length us, event | category | flops | bytes accessed | tf_op | source)
XLA Modules:
  0.0 41.9 jit_solution(16966933381368342113)
XLA Ops:
  0.0 40.2 %shard_map.37 = f32[4,8192]{1,0:T(4,128)} custom-call(bf16[16,8,8,8192]{3,2,1,0:T(8,128)(2,1)} %ens.1, s32[1,64]{1,0:T(1,128)} %active.1, s32[8]{0:T(128)} %rank.1), custom_call_target="tpu_custom_call" | custom-call | tf_op jit(solution)/shard_map/pallas_call | solution.py:360
  40.2 1.7 %copy.4 = f32[4,1,8192]{2,1,0:T(1,128)} copy(f32[4,1,8192]{2,0,1:T(4,128)} %bitcast.1) | data formatting | bytes 262144 | tf_op jit(solution)/shard_map/broadcast_in_dim | solution.py:395

commit v2 on v1

--- a/solution.py
+++ b/solution.py
@@ -17,7 +17,9 @@
 MEAN_STEP = 2.0 * FIELD_MAX / CODE_MAX
 ROOT_STEP = FIELD_MAX**0.5 / CODE_MAX
 PROB_STEP = 1.0 / CODE_MAX
-LANES = 256
+LANES = 1024
+LEAD = 2
+UNROLL = 1
 
 
 def fourth_root(x):
@@ -40,7 +42,7 @@
 
 def kernel(
     geo, ens, active, rank, out,
-    held, abuf, bbuf, sibling, own, xsend, xrecv, flags, layers, rows,
+    held, afar, anear, bfar, bnear, sibfar, sibnear, own, xsend, xrecv, flags, layers, rows,
     load_sem, asend_sem, arecv_sem, xsend_sem, xrecv_sem, fsend_sem, frecv_sem, osend_sem, orecv_sem, local_sem,
 ):
     slabs, members, bricks, pixels, depth_n, tile_n, per_tile = geo
@@ -88,44 +90,50 @@
         def _():
             greet(source_depth, jnp.int32(u))
 
-    def partial(s, side, store):
+    def partial(s, side, far, store):
         def step(i, carry):
             region = i // chunks
-            base = (region // BZ * CORES + side) * width + region % BZ * pixels
-            column = pl.multiple_of(base + i % chunks * lanes, lanes)
-            samples = [held[s, m, :, pl.ds(column, lanes)].astype(jnp.float32) for m in range(members)]
-            total = samples[0]
-            for v in samples[1:]:
-                total = total + v
-            mean = total * (1.0 / members)
-            square = None
-            above = None
-            for v in samples:
-                c = v - mean
+            chip = (x + 1 + region // BZ) % chips if far else x
+            start = (chip * CORES + side) * width + region % BZ * pixels
+            column = pl.multiple_of(start + i % chunks * lanes, lanes)
+            base = held[s, 0, :, pl.ds(column, lanes)].astype(jnp.float32)
+            total = square = None
+            above = jnp.tanh(base * (0.5 * SHARPNESS) - 0.5 * SHARPNESS * ISOVALUE)
+            for m in range(1, members):
+                v = held[s, m, :, pl.ds(column, lanes)].astype(jnp.float32)
+                above = above + jnp.tanh(v * (0.5 * SHARPNESS) - 0.5 * SHARPNESS * ISOVALUE)
+                c = v - base
+                total = c if total is None else total + c
                 c = c * c
-                h = jnp.tanh(v * (0.5 * SHARPNESS) - 0.5 * SHARPNESS * ISOVALUE)
                 square = c if square is None else square + c
-                above = h if above is None else above + h
             at = pl.ds(pl.multiple_of(i * lanes, lanes), lanes)
-            store(0, at, mean)
-            store(1, at, square * (1.0 / members))
+            shift = total * (1.0 / members)
+            store(0, at, base + shift)
+            store(1, at, jnp.maximum(square * (1.0 / members) - shift * shift, 0.0))
             store(2, at, above * (0.5 / members) + 0.5)
             return carry
 
-        lax.fori_loop(0, chips * BZ * chunks, step, 0)
-
-    def store_a(s):
+        lax.fori_loop(0, (chips - 1 if far else 1) * BZ * chunks, step, 0, unroll=UNROLL)
+
+    def store_a(s, far):
+        target = afar if far else anear
+
         def store(q, at, value):
-            abuf[s, q, :, at] = value
+            target[s, q, :, at] = value
         return store
 
-    def store_b(q, at, value):
-        bbuf[q, :, at] = value
-
-    def to_sibling(s):
+    def store_b(far):
+        target = bfar if far else bnear
+
+        def store(q, at, value):
+            target[q, :, at] = value
+        return store
+
+    def to_sibling(s, far):
+        part = 0 if far else 1
         return pltpu.make_async_remote_copy(
-            src_ref=abuf.at[s], dst_ref=sibling.at[s],
-            send_sem=asend_sem.at[s], recv_sem=arecv_sem.at[s],
+            src_ref=(afar if far else anear).at[s], dst_ref=(sibfar if far else sibnear).at[s],
+            send_sem=asend_sem.at[part, s], recv_sem=arecv_sem.at[part, s],
             device_id=(d, x * CORES + 1 - core), device_id_type=pl.DeviceIdType.MESH,
         )
 
@@ -150,42 +158,46 @@
             device_id=((d + j) % depth_n, t), device_id_type=pl.DeviceIdType.MESH,
         )
 
-    def merged(s, at):
-        ma, va, pa = (bbuf[q, :, at] for q in range(3))
+    def merged(s, far, at):
+        b, sibling = (bfar, sibfar) if far else (bnear, sibnear)
+        ma, va, pa = (b[q, :, at] for q in range(3))
         mb, vb, pb = (sibling[s, q, :, at] for q in range(3))
         gap = ma - mb
         return (ma + mb) * 0.5, (va + vb) * 0.5 + gap * gap * 0.25, (pa + pb) * 0.5
 
-    def combine(s):
-        for j in list(range(1, chips)) + [0]:
-            other = (x + j) % chips
-
-            def step(i, carry, j=j, other=other):
+    def combine_far(s):
+        for j in range(1, chips):
+            def step(i, carry, j=j):
                 at = pl.ds(pl.multiple_of(i * lanes, lanes), lanes)
                 found = []
                 for z in range(BZ):
-                    base = (other * BZ + z) * width + i * lanes
-                    found.append(merged(s, pl.ds(pl.multiple_of(base, lanes), lanes)))
-                if j == 0:
-                    for z in range(BZ):
-                        for q in range(3):
-                            own[s, z * 3 + q, :, at] = found[z][q]
-                else:
-                    (m0, v0, p0), (m1, v1, p1) = found
-                    xsend[s, j - 1, 0, :, at] = pair(
-                        to_code(m0 + FIELD_MAX, MEAN_STEP), to_code(m1 + FIELD_MAX, MEAN_STEP)
-                    )
-                    xsend[s, j - 1, 1, :, at] = pair(
-                        to_code(fourth_root(v0), ROOT_STEP), to_code(fourth_root(v1), ROOT_STEP)
-                    )
-                    xsend[s, j - 1, 2, :, at] = pair(
-                        to_code(fourth_root(p0), PROB_STEP), to_code(fourth_root(p1), PROB_STEP)
-                    )
+                    base = ((j - 1) * BZ + z) * width + i * lanes
+                    found.append(merged(s, True, pl.ds(pl.multiple_of(base, lanes), lanes)))
+                (m0, v0, p0), (m1, v1, p1) = found
+                xsend[s, j - 1, 0, :, at] = pair(
+                    to_code(m0 + FIELD_MAX, MEAN_STEP), to_code(m1 + FIELD_MAX, MEAN_STEP)
+                )
+                xsend[s, j - 1, 1, :, at] = pair(
+                    to_code(fourth_root(v0), ROOT_STEP), to_code(fourth_root(v1), ROOT_STEP)
+                )
+                xsend[s, j - 1, 2, :, at] = pair(
+                    to_code(fourth_root(p0), PROB_STEP), to_code(fourth_root(p1), PROB_STEP)
+                )
                 return carry
 
             lax.fori_loop(0, chunks, step, 0)
-            if j:
-                to_chip(s, j).start()
+            to_chip(s, j).start()
+
+    def combine_near(s):
+        def step(i, carry):
+            at = pl.ds(pl.multiple_of(i * lanes, lanes), lanes)
+            for z in range(BZ):
+                found = merged(s, False, pl.ds(pl.multiple_of(z * width + i * lanes, lanes), lanes))
+                for q in range(3):
+                    own[s, z * 3 + q, :, at] = found[q]
+            return carry
+
+        lax.fori_loop(0, chunks, step, 0)
 
     total_bricks = active.shape[1]
 
@@ -233,43 +245,57 @@
 
         lax.fori_loop(0, chunks, step, 0)
 
-    load(0).wait()
-    partial(0, 1 - core, store_a(0))
+    lead = min(LEAD, slabs)
+
+    def lead_step(s, carry):
+        load(s).wait()
+        partial(s, 1 - core, True, store_a(s, True))
+        return carry
+
+    lax.fori_loop(0, lead, lead_step, 0)
     pl.semaphore_wait(
         barrier, chips + depth_n - 1 + goals + tile_n - 2 * same.astype(jnp.int32)
     )
-    to_sibling(0).start()
+    for s in range(lead):
+        to_sibling(s, True).start()
     for j in range(1, depth_n):
         to_depth(j).start()
     mine = pltpu.make_async_copy(active, flags.at[d], local_sem.at[bricks])
     mine.start()
     mine.wait()
 
-    def slab_step(s, carry):
-        partial(s, core, store_b)
-
-        @pl.when(s < slabs - 1)
-        def _():
-            load(s + 1).wait()
-            partial(s + 1, 1 - core, store_a(s + 1))
-            to_sibling(s + 1).start()
-
-        to_sibling(s).wait_recv()
-        combine(s)
-
-        @pl.when(s == 0)
-        def _():
-            for j in range(1, depth_n):
-                from_depth(j).wait_recv()
-
-        @pl.when(s > 0)
-        def _():
-            finalize(s - 1)
-
-        return carry
-
-    lax.fori_loop(0, slabs, slab_step, 0)
-    finalize(slabs - 1)
+    def far_step(s, carry):
+        @pl.when(s < slabs - lead)
+        def _():
+            load(s + lead).wait()
+            partial(s + lead, 1 - core, True, store_a(s + lead, True))
+            to_sibling(s + lead, True).start()
+
+        partial(s, core, True, store_b(True))
+        to_sibling(s, True).wait_recv()
+        combine_far(s)
+        return carry
+
+    lax.fori_loop(0, slabs, far_step, 0)
+
+    def near_step(s, carry):
+        partial(s, 1 - core, False, store_a(s, False))
+        to_sibling(s, False).start()
+        partial(s, core, False, store_b(False))
+        to_sibling(s, False).wait_recv()
+        combine_near(s)
+        return carry
+
+    lax.fori_loop(0, slabs, near_step, 0)
+
+    for j in range(1, depth_n):
+        from_depth(j).wait_recv()
+
+    def finalize_step(s, carry):
+        finalize(s)
+        return carry
+
+    lax.fori_loop(0, slabs, finalize_step, 0)
 
     flip = rank[0]
 
@@ -334,7 +360,8 @@
                 ).wait_recv()
 
     def drain(s, carry):
-        to_sibling(s).wait_send()
+        to_sibling(s, True).wait_send()
+        to_sibling(s, False).wait_send()
         for j in range(1, chips):
             to_chip(s, j).wait_send()
         return carry
@@ -355,7 +382,8 @@
     width = pixels // tile_n
     geo = (slabs, members, bricks, pixels, depth_n, tile_n, per_tile)
     f32, i32 = jnp.float32, jnp.int32
-    side = chips * BZ * width
+    near = BZ * width
+    far = (chips - 1) * near
     dma = pltpu.SemaphoreType.DMA
     picture = pl.pallas_call(
         functools.partial(kernel, geo),
@@ -368,9 +396,12 @@
         out_specs=pl.BlockSpec(memory_space=pltpu.VMEM),
         scratch_shapes=[
             pltpu.VMEM((slabs, members, bricks, cells), jnp.bfloat16),
-            pltpu.VMEM((slabs, 3, bricks, side), f32),
-            pltpu.VMEM((3, bricks, side), f32),
-            pltpu.VMEM((slabs, 3, bricks, side), f32),
+            pltpu.VMEM((slabs, 3, bricks, far), f32),
+            pltpu.VMEM((slabs, 3, bricks, near), f32),
+            pltpu.VMEM((3, bricks, far), f32),
+            pltpu.VMEM((3, bricks, near), f32),
+            pltpu.VMEM((slabs, 3, bricks, far), f32),
+            pltpu.VMEM((slabs, 3, bricks, near), f32),
             pltpu.VMEM((slabs, 3 * BZ, bricks, width), f32),
             pltpu.VMEM((slabs, chips - 1, 3, bricks, width), i32),
             pltpu.VMEM((slabs, chips - 1, 3, bricks, width), i32),
@@ -378,8 +409,8 @@
             pltpu.VMEM((slabs, 4, bricks, width), f32),
             pltpu.VMEM((bricks, 4, width), f32),
             dma((slabs,)),
-            dma((slabs,)),
-            dma((slabs,)),
+            dma((2, slabs)),
+            dma((2, slabs)),
             dma((slabs, chips - 1)),
             dma((slabs, chips - 1)),
             dma((depth_n - 1,)),

time: 42 us -> 36 us (0.86)
  Pallas kernels: 40.2 us -> 34.1 us
    pallas_call x1, Pallas kernels: 40.2 us -> 34.1 us  [body(): pl.pallas_call(functools.partial(kernel, geo), out_shape=jax.ShapeDtypeSt...]
where the time goes in v2:
time: 36 us; the launch traced here: 35.8 us
  Pallas kernels  34.1 us (95%)
  local copies, waits for them, and re-layouts  1.69 us (5%)
    pallas_call x1, Pallas kernels, body(): pl.pallas_call(functools.partial(kernel, geo), out_shape=jax.ShapeDtypeSt...  34.1 us
    broadcast_in_dim x1, local copies, waits for them, and re-layouts, body(): return picture[:, None, :]  1.69 us

profile of v2, /device:TPU:6, one launch (start us, length us, event | category | flops | bytes accessed | tf_op | source)
XLA Modules:
  0.0 35.8 jit_solution(14380897585735538373)
XLA Ops:
  0.0 34.1 %shard_map.37 = f32[4,8192]{1,0:T(4,128)} custom-call(bf16[16,8,8,8192]{3,2,1,0:T(8,128)(2,1)} %ens.1, s32[1,64]{1,0:T(1,128)} %active.1, s32[8]{0:T(128)} %rank.1), custom_call_target="tpu_custom_call" | custom-call | tf_op jit(solution)/shard_map/pallas_call | solution.py:388
  34.1 1.7 %copy.4 = f32[4,1,8192]{2,1,0:T(1,128)} copy(f32[4,1,8192]{2,0,1:T(4,128)} %bitcast.1) | data formatting | bytes 262144 | tf_op jit(solution)/shard_map/broadcast_in_dim | solution.py:426
